TPU v7x, 32 devices: a whole 2x2x4 slice. The times are simulated.
32 devices in a mesh: dp: 4 (over z), row: 2 (over core), col: 4 (over y, x).
Axes of the slice: x: 2, y: 2, z: 4, core: 2. Of those that a mesh axis runs over, the one named last changes fastest.
Arguments:
- features: bfloat16 [2048, 4096], P(('dp', 'row')), may hold values from -6 to 6
- w_in: bfloat16 [4096, 4096], P('row', 'col'), may hold values from -0.09375 to 0.09375
- w_out: bfloat16 [4096, 1024], P('col'), may hold values from -0.09375 to 0.09375
- captions: bfloat16 [2048, 1024], P(('dp', 'row', 'col')), may hold values from -6 to 6
- positive: int32 [2048], P(('dp', 'row')), may hold values from 0 to 2047, each once
Outputs:
- fig_terms: float32 [2048], P(('dp', 'row'))
- cap_terms: float32 [2048], P(('dp', 'row', 'col'))
- grad_w_in: float32 [4096, 4096], P(('dp', 'row'), 'col')
- grad_w_out: float32 [4096, 1024], P('col', ('dp', 'row'))
Inputs may be any that keep to these rules, and one draw needn't show every extreme that they name: positive is a permutation: every caption is the match of exactly one figure.
All inputs are finite; a program needn't handle non-finite values.
Results may differ from a plain program's by a relative error of at most 0.0053.
Values may be sent and summed in bfloat16 or wider, within the bound.
A program may use at most 128 MiB of HBM per device.

v0:
```python
import jax
import jax.numpy as jnp
from jax import lax
from jax.sharding import PartitionSpec as P

SCALE = 50.0
EPS = 1e-06


def gelu_back(pre, grad):
    return jax.vjp(jax.nn.gelu, pre)[1](grad)[0]


def on_device(features, w_in, w_out, captions, positive):
    columns = features
    pre = jnp.dot(
        columns, lax.all_gather(w_in, "row", axis=0, tiled=True), preferred_element_type=jnp.float32
    )
    hidden = jax.nn.gelu(pre).astype(jnp.bfloat16)
    emb = lax.psum(jnp.dot(hidden, w_out, preferred_element_type=jnp.float32), "col")
    inv = lax.rsqrt(jnp.sum(emb * emb, axis=1, keepdims=True) + EPS)
    fhat = emb * inv
    fhat_b = fhat.astype(jnp.bfloat16)
    cap32 = captions.astype(jnp.float32)
    chat_local = (cap32 * lax.rsqrt(jnp.sum(cap32 * cap32, axis=1, keepdims=True) + EPS)).astype(
        jnp.bfloat16
    )
    block = lax.all_gather(chat_local, ("dp", "row"), axis=0, tiled=True)
    capdev = captions.shape[0]
    ncol = lax.axis_size("col")
    places = jnp.arange(block.shape[0], dtype=jnp.int32)
    colids = (places // capdev * ncol + lax.axis_index("col")) * capdev + places % capdev
    logits = SCALE * lax.dot_general(
        fhat_b, block, (((1,), (1,)), ((), ())), preferred_element_type=jnp.float32
    )
    mask = (positive[:, None] == colids[None, :]).astype(jnp.float32)
    expo = jnp.exp(logits)
    picked = mask * logits
    rowsum, rowpos = lax.psum((jnp.sum(expo, axis=1), jnp.sum(picked, axis=1)), "col")
    colsum, colpos = lax.psum((jnp.sum(expo, axis=0), jnp.sum(picked, axis=0)), ("dp", "row"))
    fig_terms = jnp.log(rowsum) - rowpos
    group = lax.axis_index("dp") * lax.axis_size("row") + lax.axis_index("row")
    cap_all = jnp.log(colsum) - colpos
    cap_terms = lax.dynamic_slice_in_dim(cap_all, group * capdev, capdev, 0)
    dlog = (expo / rowsum[:, None] + expo / colsum[None, :] - 2.0 * mask).astype(jnp.bfloat16)
    direction = SCALE * jnp.dot(dlog, block, preferred_element_type=jnp.float32)
    dfhat = lax.psum(direction, "col")
    demb = ((dfhat - fhat * jnp.sum(fhat * dfhat, axis=1, keepdims=True)) * inv).astype(
        jnp.bfloat16
    )
    dh = lax.dot_general(demb, w_out, (((1,), (1,)), ((), ())), preferred_element_type=jnp.float32)
    dpre = gelu_back(pre, dh).astype(jnp.bfloat16)
    head_term = lax.dot_general(
        hidden, demb, (((0,), (0,)), ((), ())), preferred_element_type=jnp.float32
    )
    grad_w_out = lax.psum_scatter(head_term, ("dp", "row"), scatter_dimension=1, tiled=True)
    columns = features
    grad_w_in = lax.psum_scatter(
        lax.dot_general(
            columns, dpre, (((0,), (0,)), ((), ())), preferred_element_type=jnp.float32
        ),
        ("dp", "row"),
        scatter_dimension=0,
        tiled=True,
    )
    return (fig_terms, cap_terms, grad_w_in, grad_w_out)


def solution(mesh):
    placed = (
        P(("dp", "row"), None),
        P("row", "col"),
        P("col", None),
        P(("dp", "row", "col"), None),
        P(("dp", "row")),
    )
    return jax.shard_map(
        on_device,
        mesh=mesh,
        in_specs=placed,
        out_specs=(
            P(("dp", "row")),
            P(("dp", "row", "col")),
            P(("dp", "row"), "col"),
            P("col", ("dp", "row")),
        ),
        check_vma=False,
    )
```

profile of v0, /device:TPU:0, one launch (start us, length us, event | category | flops | bytes accessed | tf_op | source)
XLA Modules:
  0.0 419.0 jit_solution(432756732322447782)
XLA Ops:
  8.0 0.0 copy-start
  8.0 0.0 all-gather.3.cloned.1.call-start
  8.1 0.7 all-gather.3.cloned.1.call-update
  8.7 0.0 all-reduce.5.cloned.1.call-start
  8.8 24.2 %all-gather.3.cloned.1.call-done = bf16[4096,1024]{1,0:T(8,128)(2,1)} async-done(((bf16[2048,1024]{1,0:T(8,128)(2,1)}), bf16[4096,1024]{1,0:T(8,128)(2,1)}) %all-gather.3.cloned.1.call-update) | async-done | bytes 8388624 | tf_op jit(solution)/shard_map/all_gather | solution.py:17
  33.0 6.3 %fusion.51 = f32[256,1024]{1,0:T(8,128)S(1)} fusion(bf16[256,4096]{1,0:T(8,128)(2,1)} %param.5, bf16[4096,1024]{1,0:T(8,128)(2,1)} %all-gather.3.cloned.1.call-done), kind=kOutput, calls=%fused_computation.72 | convolution fusion | flops 2147483648 | bytes 11534336 | tf_op jit(solution)/shard_map/dot_general | solution.py:16
  39.3 0.0 copy-start.4
  39.3 1.0 copy-done.4
  40.3 0.0 copy-done
  40.3 0.0 copy-start.5
  40.3 1.8 fusion.48
  42.1 0.0 copy-start.6
  42.1 0.0 all-reduce.5.cloned.1.call-update
  42.2 0.0 all-gather.5.cloned.1.call-start
  42.2 0.0 copy-done.5
  42.2 0.1 fusion.20
  42.4 0.8 fusion.21
  43.1 0.0 all-gather.5.cloned.1.call-update
  43.1 0.0 all-reduce.7.cloned.1.call-start
  43.2 52.8 %all-reduce.5.cloned.1.call-done = f32[256,1024]{1,0:T(8,128)} async-done(((f32[256,1024]{1,0:T(8,128)}), f32[256,1024]{1,0:T(8,128)}) %all-reduce.5.cloned.1.call-update) | async-done | bytes 1048592 | tf_op jit(solution)/shard_map/psum | solution.py:20
  96.0 1.4 multiply_reduce_fusion.1
  97.4 0.0 all-gather.5.cloned.1.call-done
  97.5 0.0 copy-done.6
  97.5 2.9 fusion.17
  100.4 16.3 %all-reduce = (f32[512]{0:T(512)S(1)}, f32[512]{0:T(512)S(1)}) all-reduce(f32[512]{0:T(512)S(1)} %get-tuple-element.8, f32[512]{0:T(512)S(1)} %get-tuple-element.10), channel_id=1, replica_groups=mesh['dp'=4,'row'=2,'col'=4] {'dp','row'}, use_global_device_ids=true, to_apply=%region_10.11 | all-reduce | flops 1024 | bytes 8192 | tf_op jit(solution)/shard_map/psum | solution.py:40
  116.7 8.9 %all-reduce.1 = (f32[256]{0:T(256)S(1)}, f32[256]{0:T(256)S(1)}) all-reduce(f32[256]{0:T(256)S(1)} %get-tuple-element.9, f32[256]{0:T(256)S(1)} %get-tuple-element.11), channel_id=1, replica_groups=mesh['dp'=4,'row'=2,'col'=4] {'col'}, use_global_device_ids=true, to_apply=%region_6.7 | all-reduce | flops 512 | bytes 4096 | tf_op jit(solution)/shard_map/psum | solution.py:39
  125.6 0.0 copy-start.1
  125.6 3.0 convolution_multiply_fusion
  128.6 0.0 all-reduce.7.cloned.1.call-update
  128.6 0.0 reduce-scatter.3.cloned.1.call-start
  128.7 49.9 %all-reduce.7.cloned.1.call-done = f32[256,1024]{1,0:T(8,128)} async-done(((f32[256,1024]{1,0:T(8,128)}), f32[256,1024]{1,0:T(8,128)}) %all-reduce.7.cloned.1.call-update) | async-done | bytes 1048592 | tf_op jit(solution)/shard_map/psum | solution.py:47
  178.6 0.0 copy-done.1
  178.6 0.0 copy-start.3
  178.6 1.6 multiply_reduce_fusion
  180.1 0.0 copy-done.3
  180.2 1.0 multiply_convert_fusion
  181.2 11.2 %convolution_bitcast_fusion = f32[4096,1024]{0,1:T(8,128)} fusion(bf16[256,4096]{1,0:T(8,128)(2,1)} %param.5, f32[256,1024]{1,0:T(8,128)} %copy-done.4, bf16[256,1024]{1,0:T(8,128)(2,1)} %multiply_convert_fusion, bf16[1024,1024]{1,0:T(8,128)(2,1)S(1)} %copy-done), kind=kOutput, calls=%fused_computation | convolution fusion | flops 2689597440 | bytes 22544384 | tf_op jit(solution)/shard_map/dot_general | solution.py:59
  192.4 0.0 copy-start.2
  192.4 0.0 reduce-scatter.3.cloned.1.call-update
  192.4 0.0 reduce-scatter.5.cloned.1.call-start
  192.5 1.0 copy-done.2
  193.5 4.0 fusion.47
  197.5 0.0 reduce-scatter.5.cloned.1.call-update
  197.5 0.6 dynamic_slice.3
  198.1 0.6 log_subtract_fusion.1
  198.7 161.9 %reduce-scatter.3.cloned.1.call-done = f32[512,1024]{0,1:T(8,128)} async-done(((f32[4096,1024]{0,1:T(8,128)}), f32[512,1024]{0,1:T(8,128)}) %reduce-scatter.3.cloned.1.call-update) | async-done | bytes 2097168 | tf_op jit(solution)/shard_map/reduce_scatter | solution.py:58
  360.6 2.9 copy.9
  363.5 48.1 %reduce-scatter.5.cloned.1.call-done = f32[1024,128]{1,0:T(8,128)} async-done(((f32[1024,1024]{1,0:T(8,128)}), f32[1024,128]{1,0:T(8,128)}) %reduce-scatter.5.cloned.1.call-update) | async-done | bytes 524304 | tf_op jit(solution)/shard_map/reduce_scatter | solution.py:56
  (4 shorter events, 0.0 us)
Async XLA Ops:
  8.0 32.3 %copy-start = (bf16[1024,1024]{1,0:T(8,128)(2,1)S(1)}, bf16[1024,1024]{1,0:T(8,128)(2,1)}, u32[]{:S(2)}) copy-start(bf16[1024,1024]{1,0:T(8,128)(2,1)} %param.7) | copy-start | bytes 6291460
  8.0 25.0 %all-gather.3.cloned.1.call-start = ((), (), s32[]{:S(2)}) async-start(), calls=%async_computation.2 | async-start | bytes 12582912 | tf_op jit(solution)/shard_map/all_gather | solution.py:17
  8.7 87.3 %all-reduce.5.cloned.1.call-start = ((), (), s32[]{:S(2)}) async-start(), calls=%async_computation.3 | async-start | bytes 2097152 | tf_op jit(solution)/shard_map/psum | solution.py:20
  39.3 1.0 copy-start.4
  40.3 1.9 copy-start.5
  42.1 55.3 %copy-start.6 = (s32[256]{0:T(256)S(1)}, s32[256]{0:T(256)}, u32[]{:S(2)}) copy-start(s32[256]{0:T(256)} %param.9) | copy-start | bytes 3076
  42.2 55.3 %all-gather.5.cloned.1.call-start = ((), (), s32[]{:S(2)}) async-start(), calls=%async_computation.4 | async-start | bytes 1179648 | tf_op jit(solution)/shard_map/all_gather | solution.py:28
  43.1 135.4 %all-reduce.7.cloned.1.call-start = ((), (), s32[]{:S(2)}) async-start(), calls=%async_computation.5 | async-start | bytes 2097152 | tf_op jit(solution)/shard_map/psum | solution.py:47
  125.6 53.0 %copy-start.1 = (f32[256,1024]{1,0:T(8,128)S(1)}, f32[256,1024]{1,0:T(8,128)}, u32[]{:S(2)}) copy-start(f32[256,1024]{1,0:T(8,128)} %all-reduce.5.cloned.1.call-done) | copy-start | bytes 3145732
  128.6 232.0 %reduce-scatter.3.cloned.1.call-start = ((), (), s32[]{:S(2)}) async-start(), calls=%async_computation.6 | async-start | bytes 18874368 | tf_op jit(solution)/shard_map/reduce_scatter | solution.py:58
  178.6 1.6 copy-start.3
  192.4 1.0 copy-start.2
  192.4 219.2 %reduce-scatter.5.cloned.1.call-start = ((), (), s32[]{:S(2)}) async-start(), calls=%async_computation.7 | async-start | bytes 4718592 | tf_op jit(solution)/shard_map/reduce_scatter | solution.py:56
Sparse Core Ops, SparseCore 0:
  10.4 22.5 all-gather.2
  42.3 53.7 all-reduce.4
  128.8 49.7 all-reduce.6
Sparse Core Ops, SparseCore 1:
  44.8 23.1 all-gather.4
  192.5 168.0 reduce-scatter.2
  363.3 48.2 reduce-scatter.4
where the time goes:
time: 419 us
  waiting for transfers between devices  338 us (81%)
  matrix products  29.3 us (7%)
  blocking collectives  25.2 us (6%)
  between operations  15.5 us (4%)
  local copies, waits for them, and re-layouts  5.45 us (1%)
  other arithmetic  5.45 us (1%)
    reduce_scatter x1, waiting for transfers between devices, on_device(): lax.psum_scatter(lax.dot_general(columns, dpre, (((0,), (0,)), ((), ())),...  162 us
    psum x1, waiting for transfers between devices, on_device(): lax.psum(jnp.dot(hidden, w_out, preferred_element_type=jnp.float32), 'col')  52.8 us
    psum x1, waiting for transfers between devices, on_device(): dfhat = lax.psum(direction, 'col')  49.9 us
    reduce_scatter x1, waiting for transfers between devices, on_device(): lax.psum_scatter(head_term, ('dp', 'row'), scatter_dimension=1, tiled=True)  48.1 us
    all_gather x1, waiting for transfers between devices, on_device(): lax.all_gather(w_in, 'row', axis=0, tiled=True)  24.2 us
    psum x1, blocking collectives, on_device(): lax.psum((jnp.sum(expo, axis=0), jnp.sum(picked, axis=0)), ('dp', 'row'))  16.3 us
    dot_general x1, matrix products, on_device(): lax.dot_general(columns, dpre, (((0,), (0,)), ((), ())), preferred_elemen...  11.2 us
    psum x1, blocking collectives, on_device(): lax.psum((jnp.sum(expo, axis=1), jnp.sum(picked, axis=1)), 'col')  8.92 us
  transfers between devices with their start and end apart: 6, of which 5 were waited for; matrix products, arithmetic and copies ran while one was open for 2% of the time, Pallas kernels for 0%

commit v1 on v0

--- a/solution.py
+++ b/solution.py
@@ -17,7 +17,9 @@
         columns, lax.all_gather(w_in, "row", axis=0, tiled=True), preferred_element_type=jnp.float32
     )
     hidden = jax.nn.gelu(pre).astype(jnp.bfloat16)
-    emb = lax.psum(jnp.dot(hidden, w_out, preferred_element_type=jnp.float32), "col")
+    field = jnp.dot(hidden, w_out, preferred_element_type=jnp.float32)
+    passed = lax.all_gather(field, axis_name="col")
+    emb = jnp.sum(passed, axis=0)
     inv = lax.rsqrt(jnp.sum(emb * emb, axis=1, keepdims=True) + EPS)
     fhat = emb * inv
     fhat_b = fhat.astype(jnp.bfloat16)

time: 419 us -> 440 us (1.050)
  waiting for transfers between devices: 338 us -> 359 us
    all_gather x0 -> x1, waiting for transfers between devices: none -> 53 us  [on_device(): passed = lax.all_gather(field, axis_name='col')]
    psum x1 -> x0, waiting for transfers between devices: 52.8 us -> none  [on_device(): lax.psum(jnp.dot(hidden, w_out, preferred_element_type=jnp.float32), 'col')]
    all_gather x1, waiting for transfers between devices: 0.02 us -> 21.4 us  [on_device(): block = lax.all_gather(chat_local, ('dp', 'row'), axis=0, tiled=True)]
  transfers between devices with their start and end apart: 6 -> 6, of which waited for: 5 -> 6; matrix products, arithmetic and copies ran while one was open for 2% -> 3% of each run, Pallas kernels for 0% -> 0%
where the time goes in v1:
time: 440 us
  waiting for transfers between devices  359 us (82%)
  matrix products  28.9 us (7%)
  blocking collectives  25.1 us (6%)
  between operations  14.2 us (3%)
  other arithmetic  6.94 us (2%)
  local copies, waits for them, and re-layouts  5.45 us (1%)
    reduce_scatter x1, waiting for transfers between devices, on_device(): lax.psum_scatter(lax.dot_general(columns, dpre, (((0,), (0,)), ((), ())),...  162 us
    all_gather x1, waiting for transfers between devices, on_device(): passed = lax.all_gather(field, axis_name='col')  53 us
    psum x1, waiting for transfers between devices, on_device(): dfhat = lax.psum(direction, 'col')  49 us
    reduce_scatter x1, waiting for transfers between devices, on_device(): lax.psum_scatter(head_term, ('dp', 'row'), scatter_dimension=1, tiled=True)  48.2 us
    all_gather x1, waiting for transfers between devices, on_device(): lax.all_gather(w_in, 'row', axis=0, tiled=True)  24.2 us
    all_gather x1, waiting for transfers between devices, on_device(): block = lax.all_gather(chat_local, ('dp', 'row'), axis=0, tiled=True)  21.4 us
    psum x1, blocking collectives, on_device(): lax.psum((jnp.sum(expo, axis=0), jnp.sum(picked, axis=0)), ('dp', 'row'))  15.4 us
    dot_general x1, matrix products, on_device(): lax.dot_general(columns, dpre, (((0,), (0,)), ((), ())), preferred_elemen...  11.2 us
  transfers between devices with their start and end apart: 6, of which 6 were waited for; matrix products, arithmetic and copies ran while one was open for 3% of the time, Pallas kernels for 0%

profile of v1, /device:TPU:0, one launch (start us, length us, event | category | flops | bytes accessed | tf_op | source)
XLA Modules:
  0.0 439.5 jit_solution(6842506910020399564)
XLA Ops:
  7.2 0.0 copy-start
  7.2 0.0 all-gather.5.cloned.1.call-start
  7.2 0.7 all-gather.5.cloned.1.call-update
  7.9 0.0 all-gather.9.cloned.1.call-start
  8.0 24.2 %all-gather.5.cloned.1.call-done = bf16[4096,1024]{1,0:T(8,128)(2,1)} async-done(((bf16[2048,1024]{1,0:T(8,128)(2,1)}), bf16[4096,1024]{1,0:T(8,128)(2,1)}) %all-gather.5.cloned.1.call-update) | async-done | bytes 8388624 | tf_op jit(solution)/shard_map/all_gather | solution.py:17
  32.1 6.3 %fusion.51 = f32[256,1024]{1,0:T(8,128)S(1)} fusion(bf16[256,4096]{1,0:T(8,128)(2,1)} %param.5, bf16[4096,1024]{1,0:T(8,128)(2,1)} %all-gather.5.cloned.1.call-done), kind=kOutput, calls=%fused_computation.72 | convolution fusion | flops 2147483648 | bytes 11534336 | tf_op jit(solution)/shard_map/dot_general | solution.py:16
  38.5 0.0 copy-start.3
  38.5 1.0 copy-done.3
  39.5 0.0 copy-done
  39.5 0.0 copy-start.4
  39.5 1.8 fusion.48
  41.3 0.0 all-gather.9.cloned.1.call-update
  41.3 0.0 all-gather.7.cloned.1.call-start
  41.4 0.0 copy-done.4
  41.4 0.1 fusion.20
  41.5 0.8 fusion.21
  42.3 0.0 all-gather.7.cloned.1.call-update
  42.3 0.0 all-reduce.4.cloned.1.call-start
  42.4 53.0 %all-gather.9.cloned.1.call-done = f32[1024,1024]{1,0:T(8,128)} async-done(((f32[256,1024]{1,0:T(8,128)}), f32[1024,1024]{1,0:T(8,128)}) %all-gather.9.cloned.1.call-update) | async-done | bytes 4194320 | tf_op jit(solution)/shard_map/all_gather | solution.py:21
  95.4 0.0 copy-start.5
  95.4 2.7 reduce_sum.72
  98.1 0.1 multiply_reduce_fusion.1
  98.2 21.4 %all-gather.7.cloned.1.call-done = bf16[512,1024]{1,0:T(8,128)(2,1)} async-done(((bf16[64,1024]{1,0:T(8,128)(2,1)}), bf16[512,1024]{1,0:T(8,128)(2,1)}) %all-gather.7.cloned.1.call-update) | async-done | bytes 1048592 | tf_op jit(solution)/shard_map/all_gather | solution.py:30
  119.7 0.0 copy-done.5
  119.7 2.6 fusion.17
  122.3 15.4 %all-reduce = (f32[512]{0:T(512)S(1)}, f32[512]{0:T(512)S(1)}) all-reduce(f32[512]{0:T(512)S(1)} %get-tuple-element.8, f32[512]{0:T(512)S(1)} %get-tuple-element.10), channel_id=1, replica_groups=mesh['dp'=4,'row'=2,'col'=4] {'dp','row'}, use_global_device_ids=true, to_apply=%region_10.11 | all-reduce | flops 1024 | bytes 8192 | tf_op jit(solution)/shard_map/psum | solution.py:42
  137.6 9.7 %all-reduce.1 = (f32[256]{0:T(256)S(1)}, f32[256]{0:T(256)S(1)}) all-reduce(f32[256]{0:T(256)S(1)} %get-tuple-element.9, f32[256]{0:T(256)S(1)} %get-tuple-element.11), channel_id=1, replica_groups=mesh['dp'=4,'row'=2,'col'=4] {'col'}, use_global_device_ids=true, to_apply=%region_6.7 | all-reduce | flops 512 | bytes 4096 | tf_op jit(solution)/shard_map/psum | solution.py:41
  147.3 2.9 convolution_multiply_fusion
  150.2 0.0 all-reduce.4.cloned.1.call-update
  150.3 0.0 reduce-scatter.3.cloned.1.call-start
  150.3 49.0 %all-reduce.4.cloned.1.call-done = f32[256,1024]{1,0:T(8,128)} async-done(((f32[256,1024]{1,0:T(8,128)}), f32[256,1024]{1,0:T(8,128)}) %all-reduce.4.cloned.1.call-update) | async-done | bytes 1048592 | tf_op jit(solution)/shard_map/psum | solution.py:49
  199.3 0.0 copy-start.2
  199.3 1.6 multiply_reduce_fusion
  200.9 0.0 copy-done.2
  200.9 1.0 multiply_convert_fusion
  201.9 11.2 %convolution_bitcast_fusion = f32[4096,1024]{0,1:T(8,128)} fusion(bf16[256,4096]{1,0:T(8,128)(2,1)} %param.5, f32[256,1024]{1,0:T(8,128)} %copy-done.3, bf16[256,1024]{1,0:T(8,128)(2,1)} %multiply_convert_fusion, bf16[1024,1024]{1,0:T(8,128)(2,1)S(1)} %copy-done), kind=kOutput, calls=%fused_computation | convolution fusion | flops 2689597440 | bytes 22544384 | tf_op jit(solution)/shard_map/dot_general | solution.py:61
  213.1 0.0 copy-start.1
  213.1 0.0 reduce-scatter.3.cloned.1.call-update
  213.2 0.0 reduce-scatter.5.cloned.1.call-start
  213.2 1.0 copy-done.1
  214.2 4.0 fusion.47
  218.2 0.0 reduce-scatter.5.cloned.1.call-update
  218.3 0.6 dynamic_slice.3
  218.9 0.6 log_subtract_fusion.1
  219.4 162.1 %reduce-scatter.3.cloned.1.call-done = f32[512,1024]{0,1:T(8,128)} async-done(((f32[4096,1024]{0,1:T(8,128)}), f32[512,1024]{0,1:T(8,128)}) %reduce-scatter.3.cloned.1.call-update) | async-done | bytes 2097168 | tf_op jit(solution)/shard_map/reduce_scatter | solution.py:60
  381.6 2.9 copy.9
  384.4 48.2 %reduce-scatter.5.cloned.1.call-done = f32[1024,128]{1,0:T(8,128)} async-done(((f32[1024,1024]{1,0:T(8,128)}), f32[1024,128]{1,0:T(8,128)}) %reduce-scatter.5.cloned.1.call-update) | async-done | bytes 524304 | tf_op jit(solution)/shard_map/reduce_scatter | solution.py:58
  (4 shorter events, 0.0 us)
Async XLA Ops:
  7.2 32.3 %copy-start = (bf16[1024,1024]{1,0:T(8,128)(2,1)S(1)}, bf16[1024,1024]{1,0:T(8,128)(2,1)}, u32[]{:S(2)}) copy-start(bf16[1024,1024]{1,0:T(8,128)(2,1)} %param.7) | copy-start | bytes 6291460
  7.2 25.0 %all-gather.5.cloned.1.call-start = ((), (), s32[]{:S(2)}) async-start(), calls=%async_computation.2 | async-start | bytes 12582912 | tf_op jit(solution)/shard_map/all_gather | solution.py:17
  7.9 87.4 %all-gather.9.cloned.1.call-start = ((), (), s32[]{:S(2)}) async-start(), calls=%async_computation.7 | async-start | bytes 5242880 | tf_op jit(solution)/shard_map/all_gather | solution.py:21
  38.5 1.0 copy-start.3
  39.5 1.9 copy-start.4
  41.3 78.3 %all-gather.7.cloned.1.call-start = ((), (), s32[]{:S(2)}) async-start(), calls=%async_computation.3 | async-start | bytes 1179648 | tf_op jit(solution)/shard_map/all_gather | solution.py:30
  42.3 157.0 %all-reduce.4.cloned.1.call-start = ((), (), s32[]{:S(2)}) async-start(), calls=%async_computation.4 | async-start | bytes 2097152 | tf_op jit(solution)/shard_map/psum | solution.py:49
  95.4 24.3 %copy-start.5 = (s32[256]{0:T(256)S(1)}, s32[256]{0:T(256)}, u32[]{:S(2)}) copy-start(s32[256]{0:T(256)} %param.9) | copy-start | bytes 3076
  150.3 231.3 %reduce-scatter.3.cloned.1.call-start = ((), (), s32[]{:S(2)}) async-start(), calls=%async_computation.5 | async-start | bytes 18874368 | tf_op jit(solution)/shard_map/reduce_scatter | solution.py:60
  199.3 1.6 copy-start.2
  213.1 1.0 copy-start.1
  213.2 219.5 %reduce-scatter.5.cloned.1.call-start = ((), (), s32[]{:S(2)}) async-start(), calls=%async_computation.6 | async-start | bytes 4718592 | tf_op jit(solution)/shard_map/reduce_scatter | solution.py:58
Sparse Core Ops, SparseCore 0:
  9.6 22.5 all-gather.4
  41.5 53.8 all-gather.8
  97.5 22.0 all-gather.6
  150.4 48.8 all-reduce.3
  213.3 168.2 reduce-scatter.2
  384.3 48.3 reduce-scatter.4
